TPU v7x, 512 devices: a whole 4x8x8 slice. The times are simulated.
512 devices in a mesh: row: 16 (over y, x_lo), col: 16 (over z, core), lag: 2 (over x_hi).
Axes of the slice: x: 4 (x_hi: 2, x_lo: 2; x = x_hi * 2 + x_lo), y: 8, z: 8, core: 2. Of those that a mesh axis runs over, the one named last changes fastest.
Arguments:
- trajectories: bfloat16 [16384, 4096], P(('row', 'col'), 'lag'), may hold values from -6 to 6
- pair_live: int32 [16, 16], replicated, may hold values from 0 to 1, as said below
Outputs:
- gram: bfloat16 [16384, 16384], P(('row', 'lag'), 'col')
Inputs may be any that keep to these rules, and one draw needn't show every extreme that they name: `pair_live`: Symmetric, with every diagonal entry 1.
All inputs are finite; a program needn't handle non-finite values.
Results may differ from a plain program's by a relative error of at most 0.0015.
Values may be sent and summed in bfloat16 or wider, within the bound.
No kernel may reach another device: no remote copies, remote signals or barrier semaphores. Data moves between devices by JAX's collectives and lax.ppermute only.
A program may use at most 64 MiB of HBM per device.

v0:
```python
import jax
import jax.numpy as jnp
from jax import lax
from jax.sharding import PartitionSpec as P


def from_root(value, axis, source):
    kept = jnp.where(lax.axis_index(axis) == source, value, 0).astype(value.dtype)
    return lax.psum(kept, axis)


def pair_distance(left, right, left_norm, right_norm):
    inner = lax.dot_general(
        left, right, (((1,), (1,)), ((), ())), preferred_element_type=jnp.float32
    )
    return left_norm[:, None] + right_norm[None, :] - 2.0 * inner


def squares(block):
    return jnp.sum(jnp.square(block.astype(jnp.float32)), axis=1)


def on_device(trajectories, pair_live):
    row_block = lax.all_gather(trajectories, "col", axis=0, tiled=True)
    col_block = from_root(row_block, "row", lax.axis_index("col"))
    live = pair_live[lax.axis_index("row"), lax.axis_index("col")]
    samples = trajectories.shape[1] * lax.axis_size("lag")
    row_norm = squares(row_block)
    col_norm = squares(col_block)
    dist = lax.psum_scatter(
        pair_distance(row_block, col_block, row_norm, col_norm),
        "lag",
        scatter_dimension=0,
        tiled=True,
    )
    gram = jnp.exp(-2.0 * dist / samples) * live.astype(jnp.float32)
    return gram.astype(jnp.bfloat16)


def solution(mesh):
    return jax.shard_map(
        on_device,
        mesh=mesh,
        in_specs=(P(("row", "col"), "lag"), P()),
        out_specs=P(("row", "lag"), "col"),
        check_vma=False,
    )
```

profile of v0, /device:TPU:1, one launch (start us, length us, event | category | flops | bytes accessed | tf_op | source)
XLA Modules:
  0.0 353.9 jit_solution(6171792190010791576)
XLA Ops:
  6.5 0.0 all-gather.2.cloned.1.call-start
  6.5 0.7 all-gather.2.cloned.1.call-update
  7.3 0.0 all-reduce.2.cloned.1.call-start
  7.3 53.8 %all-gather.2.cloned.1.call-done = bf16[1024,2048]{1,0:T(8,128)(2,1)} async-done(((bf16[64,2048]{1,0:T(8,128)(2,1)}), bf16[1024,2048]{1,0:T(8,128)(2,1)}) %all-gather.2.cloned.1.call-update) | async-done | bytes 4194320 | tf_op jit(solution)/shard_map/all_gather | solution.py:24
  61.1 2.3 broadcast_select_fusion
  63.3 0.0 all-reduce.2.cloned.1.call-update
  63.4 0.0 reduce-scatter.2.cloned.1.call-start
  63.4 3.1 multiply_reduce_fusion.1
  66.5 200.5 %all-reduce.2.cloned.1.call-done = bf16[1024,2048]{1,0:T(8,128)(2,1)} async-done(((bf16[1024,2048]{1,0:T(8,128)(2,1)}), bf16[1024,2048]{1,0:T(8,128)(2,1)}) %all-reduce.2.cloned.1.call-update) | async-done | bytes 4194320 | tf_op jit(solution)/shard_map/psum | solution.py:9
  267.0 0.0 copy-start
  267.0 3.2 multiply_reduce_fusion
  270.2 0.2 copy-done
  270.5 8.3 %bitcast_subtract_fusion = f32[1024,1024]{0,1:T(8,128)} fusion(bf16[1024,2048]{1,0:T(8,128)(2,1)} %all-reduce.2.cloned.1.call-done, bf16[1024,2048]{1,0:T(8,128)(2,1)S(1)} %copy-done, f32[1024]{0:T(1024)S(1)} %multiply_reduce_fusion, f32[1024]{0:T(1024)S(1)} %multiply_reduce_fusion.1), kind=kOutput, calls=%fused_computation.2 | convolution fusion | flops 4298113024 | bytes 12591104 | tf_op jit(solution)/shard_map/dot_general | solution.py:13
  278.8 0.0 reduce-scatter.2.cloned.1.call-update
  278.8 1.3 dynamic_slice.3
  280.7 63.4 %reduce-scatter.2.cloned.1.call-done = f32[512,1024]{0,1:T(8,128)} async-done(((f32[1024,1024]{0,1:T(8,128)}), f32[512,1024]{0,1:T(8,128)}) %reduce-scatter.2.cloned.1.call-update) | async-done | bytes 2097168 | tf_op jit(solution)/shard_map/reduce_scatter | solution.py:30
  344.1 1.9 multiply_convert_fusion
  346.0 1.3 copy.3
Async XLA Ops:
  6.5 54.6 %all-gather.2.cloned.1.call-start = ((), (), s32[]{:S(2)}) async-start(), calls=%async_computation.1 | async-start | bytes 4456448 | tf_op jit(solution)/shard_map/all_gather | solution.py:24
  7.3 259.8 %all-reduce.2.cloned.1.call-start = ((), (), s32[]{:S(2)}) async-start(), calls=%async_computation.2 | async-start | bytes 8388608 | tf_op jit(solution)/shard_map/psum | solution.py:9
  63.4 280.7 %reduce-scatter.2.cloned.1.call-start = ((), (), s32[]{:S(2)}) async-start(), calls=%async_computation.3 | async-start | bytes 6291456 | tf_op jit(solution)/shard_map/reduce_scatter | solution.py:30
  267.0 3.4 copy-start
Sparse Core Ops, SparseCore 0:
  9.5 51.5 all-gather.1
  64.0 202.9 all-reduce.1
  278.9 65.1 reduce-scatter.1
where the time goes:
time: 354 us
  waiting for transfers between devices  318 us (90%)
  between operations  13.8 us (4%)
  other arithmetic  10.5 us (3%)
  matrix products  8.28 us (2%)
    psum x1, waiting for transfers between devices, from_root(): return lax.psum(kept, axis)  201 us
    reduce_scatter x1, waiting for transfers between devices, on_device(): lax.psum_scatter(pair_distance(row_block, col_block, row_norm, col_norm),...  63.4 us
    all_gather x1, waiting for transfers between devices, on_device(): row_block = lax.all_gather(trajectories, 'col', axis=0, tiled=True)  53.8 us
    dot_general x1, matrix products, pair_distance(): lax.dot_general(left, right, (((1,), (1,)), ((), ())), preferred_element_...  8.28 us
  transfers between devices with their start and end apart: 3, of which 3 were waited for; matrix products, arithmetic and copies ran while one was open for 1% of the time, Pallas kernels for 0%

commit v1 on v0

--- a/solution.py
+++ b/solution.py
@@ -21,7 +21,9 @@
 
 
 def on_device(trajectories, pair_live):
-    row_block = lax.all_gather(trajectories, "col", axis=0, tiled=True)
+    row_block = jnp.concatenate(
+        lax.all_to_all(jnp.stack([trajectories] * lax.axis_size("col")), "col", 0, 0), axis=0
+    )
     col_block = from_root(row_block, "row", lax.axis_index("col"))
     live = pair_live[lax.axis_index("row"), lax.axis_index("col")]
     samples = trajectories.shape[1] * lax.axis_size("lag")

time: 354 us -> 410 us (1.16)
  waiting for transfers between devices: 318 us -> 357 us
  starting transfers between devices: 0.08 us -> 11.9 us
    all_to_all x0 -> x1, waiting for transfers between devices: none -> 93.5 us  [on_device(): lax.all_to_all(jnp.stack([trajectories] * lax.axis_size('col')), 'col', 0...]
    all_gather x1 -> x0, waiting for transfers between devices: 53.8 us -> none  [on_device(): row_block = lax.all_gather(trajectories, 'col', axis=0, tiled=True)]
    all_to_all x0 -> x1, starting transfers between devices: none -> 11.8 us  [on_device(): lax.all_to_all(jnp.stack([trajectories] * lax.axis_size('col')), 'col', 0...]
where the time goes in v1:
time: 410 us
  waiting for transfers between devices  357 us (87%)
  between operations  14.1 us (3%)
  other arithmetic  12.6 us (3%)
  starting transfers between devices  11.9 us (3%)
  matrix products  8.29 us (2%)
  local copies, waits for them, and re-layouts  6.33 us (2%)
    psum x1, waiting for transfers between devices, from_root(): return lax.psum(kept, axis)  200 us
    all_to_all x1, waiting for transfers between devices, on_device(): lax.all_to_all(jnp.stack([trajectories] * lax.axis_size('col')), 'col', 0...  93.5 us
    reduce_scatter x1, waiting for transfers between devices, on_device(): lax.psum_scatter(pair_distance(row_block, col_block, row_norm, col_norm),...  63.4 us
    all_to_all x1, starting transfers between devices, on_device(): lax.all_to_all(jnp.stack([trajectories] * lax.axis_size('col')), 'col', 0...  11.8 us
    dot_general x1, matrix products, pair_distance(): lax.dot_general(left, right, (((1,), (1,)), ((), ())), preferred_element_...  8.29 us
  transfers between devices with their start and end apart: 3, of which 3 were waited for; matrix products, arithmetic and copies ran while one was open for 1% of the time, Pallas kernels for 0%

profile of v1, /device:TPU:1, one launch (start us, length us, event | category | flops | bytes accessed | tf_op | source)
XLA Modules:
  0.0 410.1 jit_solution(15486271560886033314)
XLA Ops:
  6.5 3.4 stack.2
  10.0 11.8 %all-to-all-start = ((bf16[16,64,2048]{2,1,0:T(8,128)(2,1)}), bf16[16,64,2048]{2,1,0:T(8,128)(2,1)}, u32[]{:S(2)}, u32[]{:S(2)}) async-start(bf16[16,64,2048]{2,1,0:T(8,128)(2,1)} %stack.2), calls=%async_computation | async-start | bytes 8388608 | tf_op jit(solution)/shard_map/all_to_all | solution.py:25
  21.8 0.0 all-reduce.2.cloned.1.call-start
  21.9 93.5 %all-to-all-done = bf16[16,64,2048]{2,1,0:T(8,128)(2,1)} async-done(((bf16[16,64,2048]{2,1,0:T(8,128)(2,1)}), bf16[16,64,2048]{2,1,0:T(8,128)(2,1)}, u32[]{:S(2)}, u32[]{:S(2)}) %all-to-all-start) | async-done | bytes 4194336 | tf_op jit(solution)/shard_map/all_to_all | solution.py:25
  115.4 4.4 %broadcast_select_fusion = bf16[1024,2048]{1,0:T(8,128)(2,1)} fusion(pred[]{:T(512)S(6)} %eq.3, bf16[16,64,2048]{2,1,0:T(8,128)(2,1)} %all-to-all-done), kind=kLoop, calls=%fused_computation.3 | loop fusion | flops 2097152 | bytes 8388609 | tf_op jit(solution)/shard_map/jit(_where)/select_n | solution.py:8
  119.8 0.0 all-reduce.2.cloned.1.call-update
  119.9 0.0 reduce-scatter.2.cloned.1.call-start
  119.9 3.1 multiply_reduce_fusion.1
  123.0 0.1 add.25
  123.1 199.8 %all-reduce.2.cloned.1.call-done = bf16[1024,2048]{1,0:T(8,128)(2,1)} async-done(((bf16[1024,2048]{1,0:T(8,128)(2,1)}), bf16[1024,2048]{1,0:T(8,128)(2,1)}) %all-reduce.2.cloned.1.call-update) | async-done | bytes 4194320 | tf_op jit(solution)/shard_map/psum | solution.py:9
  322.9 0.0 copy-start
  322.9 3.2 multiply_reduce_fusion
  326.1 0.2 copy-done
  326.3 8.3 %bitcast_subtract_fusion = f32[1024,1024]{0,1:T(8,128)} fusion(bf16[1024,2048]{1,0:T(8,128)(2,1)S(1)} %copy-done, bf16[1024,2048]{1,0:T(8,128)(2,1)} %bitcast, f32[1024]{0:T(1024)S(1)} %multiply_reduce_fusion, f32[1024]{0:T(1024)S(1)} %add.25), kind=kOutput, calls=%fused_computation.2 | convolution fusion | flops 4298113024 | bytes 12591104 | tf_op jit(solution)/shard_map/dot_general | solution.py:13
  334.6 0.0 reduce-scatter.2.cloned.1.call-update
  334.6 1.3 dynamic_slice.3
  336.6 63.4 %reduce-scatter.2.cloned.1.call-done = f32[512,1024]{0,1:T(8,128)} async-done(((f32[1024,1024]{0,1:T(8,128)}), f32[512,1024]{0,1:T(8,128)}) %reduce-scatter.2.cloned.1.call-update) | async-done | bytes 2097168 | tf_op jit(solution)/shard_map/reduce_scatter | solution.py:32
  400.0 1.9 multiply_convert_fusion
  401.9 1.3 copy.4
Async XLA Ops:
  10.0 105.4 %all-to-all-start = ((bf16[16,64,2048]{2,1,0:T(8,128)(2,1)}), bf16[16,64,2048]{2,1,0:T(8,128)(2,1)}, u32[]{:S(2)}, u32[]{:S(2)}) async-start(bf16[16,64,2048]{2,1,0:T(8,128)(2,1)} %stack.2), calls=%async_computation | async-start | bytes 8388608 | tf_op jit(solution)/shard_map/all_to_all | solution.py:25
  21.8 301.1 %all-reduce.2.cloned.1.call-start = ((), (), s32[]{:S(2)}) async-start(), calls=%async_computation.2 | async-start | bytes 8388608 | tf_op jit(solution)/shard_map/psum | solution.py:9
  119.9 280.1 %reduce-scatter.2.cloned.1.call-start = ((), (), s32[]{:S(2)}) async-start(), calls=%async_computation.3 | async-start | bytes 6291456 | tf_op jit(solution)/shard_map/reduce_scatter | solution.py:32
  322.9 3.4 copy-start
Sparse Core Ops, SparseCore 0:
  120.0 202.8 all-reduce.1
  334.8 65.1 reduce-scatter.1
